TPU v7x, 128 devices: a whole 4x4x4 slice. The times are simulated.
128 devices in a mesh: ctx: 32 (over z_hi, y, x), tp: 4 (over z_lo, core).
Axes of the slice: x: 4, y: 4, z: 4 (z_hi: 2, z_lo: 2; z = z_hi * 2 + z_lo), core: 2. Of those that a mesh axis runs over, the one named last changes fastest.
Arguments:
- tokens: bfloat16 [49152, 4096], P(('ctx', 'tp')), may hold values from -8 to 8
- norm_gain: bfloat16 [4096], replicated, may hold values from 0.25 to 1.75
- w_in: bfloat16 [4096, 3, 2048], P(None, None, 'tp'), may hold values from -0.09375 to 0.09375
- short_weight: bfloat16 [7, 3, 2048], P(None, None, 'tp'), may hold values from -2 to 2
- conv_bias: float32 [2048], P('tp'), may hold values from -4 to 4
- decay_rates: float32 [16, 2048], P(None, 'tp'), may hold values from 0 to 1, as said below
- residues: float32 [16, 2048], P(None, 'tp'), may hold values from -1.5 to 1.5
- w_out: bfloat16 [2048, 4096], P('tp'), may hold values from -0.125 to 0.125
Outputs:
- mixed: bfloat16 [49152, 4096], P(('ctx', 'tp'))
Inputs may be any that keep to these rules, and one draw needn't show every extreme that they name: `decay_rates`: every rate lies between 1 / 98304 and 1/30.
All inputs are finite; a program needn't handle non-finite values.
Results may differ from a plain program's by a relative error of at most 0.015.
Values may be sent and summed in bfloat16 or wider, within the bound.
A program may use at most 192 MiB of HBM per device.

v0:
```python
import jax
import jax.numpy as jnp
from jax import lax
from jax.sharding import PartitionSpec as P

highest_precision = lax.Precision.HIGHEST


def short_filter(padded, tap_weights):
    tap_count = tap_weights.shape[0]
    length = padded.shape[-1] - (tap_count - 1)
    summed = jnp.zeros(padded.shape[:-1] + (length,), jnp.float32)
    for tap_index in range(tap_count):
        offset = tap_count - 1 - tap_index
        summed = (
            summed
            + tap_weights[tap_index].astype(jnp.float32)[:, :, None]
            * padded[:, :, offset : offset + length]
        )
    return summed


def long_filter(product, decays, residue_part, bias_part):
    chan_count, length = product.shape
    block_len = min(512, length)
    block_count = length // block_len
    widened = product.astype(jnp.float32)
    signal = widened.reshape(chan_count, block_count, block_len)
    rate_cols = decays.T
    weight_cols = (residue_part * jnp.sqrt(2.0 * decays)).T
    offsets = jnp.arange(block_len, dtype=jnp.float32)
    falling = weight_cols[:, None, :] * jnp.exp(-rate_cols[:, None, :] * offsets[None, :, None])
    rising = jnp.exp(rate_cols[:, None, :] * offsets[None, :, None])
    toeplitz = jnp.einsum("cir,cjr->cij", falling, rising, precision=highest_precision)
    below_diag = offsets[:, None] >= offsets[None, :]
    toeplitz = jnp.where(below_diag[None], toeplitz, 0.0)
    within_block = jnp.einsum("cij,cnj->cni", toeplitz, signal, precision=highest_precision)
    closing = jnp.exp(-rate_cols[:, :, None] * (block_len - 1.0 - offsets)[None, None, :])
    block_ends = jnp.einsum("crj,cnj->crn", closing, signal, precision=highest_precision)
    block_steps = jnp.arange(block_count)
    block_gap = block_steps[:, None] - 1 - block_steps[None, :]
    gap_float = jnp.maximum(block_gap, 0).astype(jnp.float32)
    carried = jnp.exp(-rate_cols[:, :, None, None] * (block_len * gap_float)[None, None])
    carried = jnp.where((block_gap >= 0)[None, None], carried, 0.0)
    states = jnp.einsum("crnm,crm->crn", carried, block_ends, precision=highest_precision)
    opening = weight_cols[:, :, None] * jnp.exp(
        -rate_cols[:, :, None] * (offsets + 1.0)[None, None, :]
    )
    from_before = jnp.einsum("cri,crn->cni", opening, states, precision=highest_precision)
    return (within_block + from_before).reshape(chan_count, length) + bias_part[:, None] * widened


def shards(tokens, norm_gain, w_in, short_weight, conv_bias, decay_rates, residues, w_out):
    widened = tokens.astype(jnp.float32)
    normed = (
        widened
        * lax.rsqrt(jnp.mean(widened * widened, axis=1, keepdims=True) + 1e-06)
        * norm_gain.astype(jnp.float32)
    ).astype(jnp.bfloat16)
    model_width = w_in.shape[0]
    shard_chans = w_in.shape[2]
    flat_in = w_in.reshape(model_width, 3 * shard_chans)
    projected = lax.dot_general(
        flat_in,
        lax.all_gather(normed, "tp", axis=0, tiled=True),
        (((0,), (1,)), ((), ())),
        preferred_element_type=jnp.float32,
    ).astype(jnp.bfloat16)
    local_length = projected.shape[1]
    streams = projected.reshape(3, shard_chans, local_length)
    ctx_count = lax.axis_size("ctx")
    chan_count = shard_chans // ctx_count
    first_chan = lax.axis_index("ctx") * chan_count
    decays = lax.dynamic_slice_in_dim(decay_rates, first_chan, chan_count, 1)
    residue_part = lax.dynamic_slice_in_dim(residues, first_chan, chan_count, 1)
    bias_part = lax.dynamic_slice_in_dim(conv_bias, first_chan, chan_count, 0)
    tap_count = short_weight.shape[0]
    moved = lax.all_to_all(streams, "ctx", split_axis=1, concat_axis=2, tiled=True)
    tap_part = lax.dynamic_slice_in_dim(short_weight, first_chan, chan_count, 2)
    padded = jnp.pad(moved.astype(jnp.float32), ((0, 0), (0, 0), (tap_count - 1, 0)))
    filtered = short_filter(padded, tap_part)
    product = lax.optimization_barrier((filtered[1] * filtered[2]).astype(jnp.bfloat16))
    convolved = lax.optimization_barrier(
        long_filter(product, decays, residue_part, bias_part).astype(jnp.bfloat16)
    )
    returned = (filtered[0] * convolved.astype(jnp.float32)).astype(jnp.bfloat16)
    arrived = lax.all_to_all(returned, "ctx", split_axis=1, concat_axis=0, tiled=True)
    partial_value = lax.dot_general(
        arrived, w_out, (((0,), (0,)), ((), ())), preferred_element_type=jnp.float32
    )
    summed = lax.psum_scatter(
        lax.optimization_barrier(partial_value.astype(jnp.bfloat16))
        .astype(jnp.float32)
        .astype(jnp.bfloat16),
        "tp",
        scatter_dimension=0,
        tiled=True,
    ).astype(jnp.float32)
    return (widened + summed).astype(jnp.bfloat16)


def solution(mesh):
    in_specs = (
        P(("ctx", "tp"), None),
        P(),
        P(None, None, "tp"),
        P(None, None, "tp"),
        P("tp"),
        P(None, "tp"),
        P(None, "tp"),
        P("tp", None),
    )
    out_specs = P(("ctx", "tp"), None)
    return jax.shard_map(shards, mesh=mesh, in_specs=in_specs, out_specs=out_specs, check_vma=False)
```

profile of v0, /device:TPU:1, one launch (start us, length us, event | category | flops | bytes accessed | tf_op | source)
XLA Modules:
  0.0 568.7 jit_solution(16156391126312856001)
XLA Ops:
  7.2 2.6 fusion.8
  9.8 4.6 fusion.10
  14.5 17.2 %copy.33 = bf16[4096,3,512]{0,2,1:T(8,128)(2,1)} copy(bf16[4096,3,512]{2,0,1:T(8,128)(2,1)} %param.10) | data formatting | bytes 25165824 | tf_op args[2]
  31.7 102.9 %all-gather.2.cloned.1.call-done = bf16[1536,4096]{1,0:T(8,128)(2,1)} async-done(((bf16[384,4096]{1,0:T(8,128)(2,1)}), bf16[1536,4096]{1,0:T(8,128)(2,1)}) %all-gather.2.cloned.1.call-update) | async-done | bytes 12582928 | tf_op jit(solution)/shard_map/all_gather | solution.py:65
  134.6 25.9 %convolution_convert_fusion.1 = bf16[1536,1536]{0,1:T(8,128)(2,1)S(1)} fusion(bf16[1536,4096]{1,0:T(8,128)(2,1)} %all-gather.2.cloned.1.call-done, bf16[4096,1536]{0,1:T(8,128)(2,1)} %bitcast.65), kind=kOutput, calls=%fused_computation.14 | convolution fusion | flops 19329712128 | bytes 29884416 | tf_op jit(solution)/shard_map/dot_general | solution.py:63
  160.6 6.7 %copy.34 = bf16[3,512,1536]{2,0,1:T(4,128)(2,1)} copy(bf16[3,512,1536]{2,1,0:T(8,128)(2,1)S(1)} %bitcast.70) | data formatting | bytes 9437184 | tf_op jit(solution)/shard_map/reshape | solution.py:70
  167.3 9.5 %all-to-all-start = ((bf16[3,512,1536]{2,0,1:T(4,128)(2,1)}), bf16[3,512,1536]{2,0,1:T(4,128)(2,1)}, u32[]{:S(2)}, u32[]{:S(2)}) async-start(bf16[3,512,1536]{2,0,1:T(4,128)(2,1)} %copy.34), calls=%async_computation | async-start | bytes 12582912 | tf_op jit(solution)/shard_map/all_to_all | solution.py:78
  180.2 16.8 %fusion.26 = f32[16,512,512]{2,1,0:T(8,128)} fusion(f32[16,16]{1,0:T(8,128)S(1)} %copy.38, f32[16,16]{1,0:T(8,128)S(1)} %copy.37, f32[16,16]{1,0:T(8,128)S(1)} %copy.36), kind=kOutput, calls=%fused_computation.39 | convolution fusion | flops 805699584 | bytes 16780288 | tf_op jit(solution)/shard_map/cir,cjr->cij/dot_general | solution.py:34
  197.0 72.7 %all-to-all-done = bf16[3,512,1536]{2,0,1:T(4,128)(2,1)} async-done(((bf16[3,512,1536]{2,0,1:T(4,128)(2,1)}), bf16[3,512,1536]{2,0,1:T(4,128)(2,1)}, u32[]{:S(2)}, u32[]{:S(2)}) %all-to-all-start) | async-done | bytes 4718624 | tf_op jit(solution)/shard_map/all_to_all | solution.py:78
  269.7 9.3 %convert_bitcast_fusion = f32[3,16,32,1536]{3,0,1,2:T(4,128)} fusion(bf16[3,32,16,1536]{3,0,2,1:T(4,128)(2,1)} %bitcast.16), kind=kLoop, calls=%fused_computation.3 | loop fusion | flops 2359296 | bytes 14155776 | tf_op jit(solution)/shard_map/convert_element_type | solution.py:80
  279.0 13.7 %copy.35 = f32[3,16,32,1536]{3,2,1,0:T(8,128)} copy(f32[3,16,32,1536]{3,0,1,2:T(4,128)} %convert_bitcast_fusion) | data formatting | bytes 18874368 | tf_op jit(solution)/shard_map/convert_element_type | solution.py:80
  292.7 9.2 %reshape.159 = f32[3,16,49152]{2,1,0:T(8,128)} reshape(f32[3,16,32,1536]{3,2,1,0:T(8,128)} %copy.35) | data formatting | bytes 18874368 | tf_op jit(solution)/shard_map/convert_element_type | solution.py:80
  301.8 35.3 %multiply_add_fusion = f32[3,16,49152]{2,1,0:T(8,128)} fusion(f32[3,16,49152]{2,1,0:T(8,128)} %reshape.159, f32[3,16]{1,0:T(4,128)S(1)} %get-tuple-element.14, f32[3,16]{1,0:T(4,128)S(1)} %get-tuple-element.15, f32[3,16]{1,0:T(4,128)S(1)} %get-tuple-element.16, f32[3,16]{1,0:T(4,128)S(1)} %get-tuple-element.17, f32[3,16]{1,0:T(4,128)S(1)} %get-tuple-element.18, ...), kind=kLoop, calls=%fused_computation.11 | loop fusion | flops 30670848 | bytes 18875712 | tf_op jit(solution)/shard_map/add | solution.py:16
  337.1 3.1 fusion.19
  340.8 1.4 fusion.23
  342.1 13.4 %fusion = f32[16,96,512]{2,1,0:T(8,128)S(1)} fusion(bf16[16,96,512]{2,1,0:T(8,128)(2,1)S(1)} %bitcast.64, f32[16,512,512]{2,1,0:T(8,128)} %fusion.26, pred[512,512]{1,0:T(8,128)(4,1)S(1)} %iota_compare_fusion), kind=kOutput, calls=%fused_computation | convolution fusion | flops 4836032512 | bytes 21757952 | tf_op jit(solution)/shard_map/cij,cnj->cni/dot_general | solution.py:37
  355.5 33.8 %fusion.2 = f32[16,16,1,96]{3,2,1,0:T(1,128)S(1)} fusion(f32[16,16,96,1]{2,3,1,0:T(1,128)S(1)} %bitcast.73, f32[96,96]{1,0:T(8,128)S(1)} %convert_multiply_fusion.2, f32[16,16]{1,0:T(8,128)S(1)} %copy.37, pred[96,96]{1,0:T(8,128)(4,1)S(1)} %fusion.42), kind=kOutput, calls=%fused_computation.4 | convolution fusion | flops 33030144 | bytes 243712 | tf_op jit(solution)/shard_map/crnm,crm->crn/dot_general | solution.py:45
  389.3 2.8 convolution_add_fusion
  392.2 1.8 copy.54
  394.5 2.3 fusion.18
  397.0 33.7 %all_to_all.28 = bf16[16,32,1536]{2,0,1:T(8,128)(2,1)S(1)} all-to-all(bf16[16,32,1536]{2,0,1:T(8,128)(2,1)S(1)} %bitcast.68), channel_id=1, replica_groups=mesh['ctx'=32,'tp'=4] {'ctx'}, dimensions={1} | all-to-all | bytes 3145728 | tf_op jit(solution)/shard_map/all_to_all | solution.py:87
  430.7 9.7 %convolution_convert_fusion = bf16[1536,4096]{1,0:T(8,128)(2,1)} fusion(bf16[512,1536]{1,0:T(8,128)(2,1)S(1)} %bitcast.71, bf16[512,4096]{1,0:T(8,128)(2,1)S(1)} %copy-done.2), kind=kOutput, calls=%fused_computation.2 | convolution fusion | flops 6448742400 | bytes 18350080 | tf_op jit(solution)/shard_map/dot_general | solution.py:88
  440.4 116.3 %reduce-scatter.2.cloned.1.call-done = bf16[384,4096]{1,0:T(8,128)(2,1)} async-done(((bf16[1536,4096]{1,0:T(8,128)(2,1)}), bf16[384,4096]{1,0:T(8,128)(2,1)}) %reduce-scatter.2.cloned.1.call-update) | async-done | bytes 3145744 | tf_op jit(solution)/shard_map/reduce_scatter | solution.py:91
  556.7 4.7 fusion.11
  (32 shorter events, 5.2 us)
Async XLA Ops:
  6.5 128.1 %all-gather.2.cloned.1.call-start = ((), (), s32[]{:S(2)}) async-start(), calls=%async_computation.3 | async-start | bytes 15728640 | tf_op jit(solution)/shard_map/all_gather | solution.py:65
  167.3 10.7 %copy-start.1 = (f32[16,512]{1,0:T(8,128)S(1)}, f32[16,512]{1,0:T(8,128)}, u32[]{:S(2)}) copy-start(f32[16,512]{1,0:T(8,128)} %param.13) | copy-start | bytes 98308
  167.3 102.4 %all-to-all-start = ((bf16[3,512,1536]{2,0,1:T(4,128)(2,1)}), bf16[3,512,1536]{2,0,1:T(4,128)(2,1)}, u32[]{:S(2)}, u32[]{:S(2)}) async-start(bf16[3,512,1536]{2,0,1:T(4,128)(2,1)} %copy.34), calls=%async_computation | async-start | bytes 12582912 | tf_op jit(solution)/shard_map/all_to_all | solution.py:78
  176.8 379.9 %reduce-scatter.2.cloned.1.call-start = ((), (), s32[]{:S(2)}) async-start(), calls=%async_computation.4 | async-start | bytes 15728640 | tf_op jit(solution)/shard_map/reduce_scatter | solution.py:91
  394.5 36.2 %copy-start.2 = (bf16[512,4096]{1,0:T(8,128)(2,1)S(1)}, bf16[512,4096]{1,0:T(8,128)(2,1)}, u32[]{:S(2)}) copy-start(bf16[512,4096]{1,0:T(8,128)(2,1)} %param.15) | copy-start | bytes 12582916
  440.3 116.3 %copy-start = (bf16[384,4096]{1,0:T(8,128)(2,1)S(1)}, bf16[384,4096]{1,0:T(8,128)(2,1)}, u32[]{:S(2)}) copy-start(bf16[384,4096]{1,0:T(8,128)(2,1)} %param.8) | copy-start | bytes 9437188
Sparse Core Ops, SparseCore 0:
  14.6 119.9 all-gather.1
  440.5 116.1 reduce-scatter.1
where the time goes:
time: 578 us; the launch traced here: 569 us
  waiting for transfers between devices  292 us (51%)
  matrix products  104 us (18%)
  other arithmetic  65.4 us (11%)
  local copies, waits for them, and re-layouts  50.3 us (9%)
  blocking collectives  33.7 us (6%)
  between operations  14 us (2%)
  starting transfers between devices  9.57 us (2%)
    reduce_scatter x1, waiting for transfers between devices, shards(): lax.psum_scatter(lax.optimization_barrier(partial_value.astype(jnp.bfloat...  116 us
    all_gather x1, waiting for transfers between devices, shards(): lax.all_gather(normed, 'tp', axis=0, tiled=True)  103 us
    all_to_all x1, waiting for transfers between devices, shards(): lax.all_to_all(streams, 'ctx', split_axis=1, concat_axis=2, tiled=True)  72.7 us
    add x1, other arithmetic, short_filter(): summed + tap_weights[tap_index].astype(jnp.float32)[:, :, None] * padded[...  35.3 us
    dot_general x1, matrix products, long_filter(): jnp.einsum('crnm,crm->crn', carried, block_ends, precision=highest_precis...  33.8 us
    all_to_all x1, blocking collectives, shards(): lax.all_to_all(returned, 'ctx', split_axis=1, concat_axis=0, tiled=True)  33.7 us
    dot_general x1, matrix products, shards(): lax.dot_general(flat_in, lax.all_gather(normed, 'tp', axis=0, tiled=True)...  25.9 us
    convert_element_type x2, local copies, waits for them, and re-layouts, shards(): moved.astype(jnp.float32)  22.9 us
  transfers between devices with their start and end apart: 3, of which 3 were waited for; matrix products, arithmetic and copies ran while one was open for 7% of the time, Pallas kernels for 0%

commit v1 on v0

v1 whole, which is shorter than its diff:
```python
import functools

import jax
import jax.numpy as jnp
from jax import lax
from jax.experimental import pallas as pl
from jax.experimental.pallas import tpu as pltpu
from jax.sharding import PartitionSpec as P

MESH = pl.DeviceIdType.MESH
BF, F32 = jnp.bfloat16, jnp.float32

ROWS = 384
HALO = 16
SLOT = ROWS + HALO
WIDTH = 4096
CH = 512
CHUNKS = 5
CROWS = SLOT // CHUNKS
ORDER = (1, 0, 2, 3, 4)
PIECES = 8
STEPS = ROWS // PIECES
MODES = 16
TAPS = 7
LG = CH // 128
STATE = F32
UNROLL = 6

S_HALO = 0
S_XZ = 1
S_XD = S_XZ + CHUNKS
S_XF = S_XD + CHUNKS
S_WZ = S_XF + CHUNKS
S_WD = S_WZ + 2
S_WA = S_WD + 1
S_WB = S_WA + 6
S_WC = S_WB + 6
S_E1 = S_WC + 1
S_E2 = S_E1 + 7
S_G = S_E2 + 3
S_N = S_G + 3
L_TOK = 0
L_WIN = CHUNKS
L_WO = L_WIN + 3
L_RES = L_WO + 1
L_OUT = L_RES + 1
OUT_TILES = 8
L_N = L_OUT + OUT_TILES
OUT_COLS = WIDTH // OUT_TILES


def kernel(
    tok, gain, w3, taps, bias, decay, resid, w_out, out,
    xo, xr, wi, wo, proj, gs, gg, tapb, ab, wb, lb, bb, lam, xe, et, sin, r1, r2, ss, rs, ls,
):
    ctx = lax.axis_index("ctx")
    tp = lax.axis_index("tp")
    x = lax.rem(ctx, 4)
    y = lax.rem(lax.div(ctx, 4), 4)
    h = lax.div(ctx, 16)
    p = lax.div(tp, 2)
    k = lax.rem(tp, 2)
    z = 2 * h + p
    s = 2 * k - 1

    def dev(dx, dy, dz, core):
        zz = lax.rem(dz + 4, 4)
        return (lax.div(zz, 2) * 16 + lax.rem(dy, 4) * 4 + lax.rem(dx, 4), lax.rem(zz, 2) * 2 + core)

    order_at = ctx * 4 + tp
    nxt = lax.rem(order_at + 1, 128)
    prv = lax.rem(order_at + 127, 128)
    nxt = (lax.div(nxt, 4), lax.rem(nxt, 4))
    prv = (lax.div(prv, 4), lax.rem(prv, 4))
    other = dev(x, y, z, 1 - k)
    partner = dev(x, y, z + s, 1 - k)
    gate_to = dev(x, y, z - s, k)
    gate_from = dev(x, y, z + s, k)
    x_peers = [dev(x + d, y, z, k) for d in (1, 2, 3)]
    y_peers = [dev(x, y + d, z, k) for d in (1, 2, 3)]
    line_at = h * 4 + x
    line_peers = []
    for d in range(1, 8):
        at = lax.rem(line_at + d, 8)
        line_peers.append((lax.div(at, 4) * 16 + y * 4 + lax.rem(at, 4), tp))
    own_j = 2 * p + k
    oth_j = 2 * p + 1 - k
    far_j = 2 * (1 - p) + 1 - k
    far2_j = 2 * (1 - p) + k

    def remote(src, dst, at, to):
        return pltpu.make_async_remote_copy(
            src_ref=src, dst_ref=dst, send_sem=ss.at[at], recv_sem=rs.at[at], device_id=to, device_id_type=MESH
        )

    def local(src, dst, at):
        return pltpu.make_async_copy(src, dst, ls.at[at])

    tok_copies = {}
    for c in ORDER:
        first = 0 if c == 0 else c * CROWS - HALO
        count = CROWS - HALO if c == 0 else CROWS
        tok_copies[c] = local(tok.at[pl.ds(first, count)], xo.at[k, pl.ds(first + HALO, count)], L_TOK + c)
        tok_copies[c].start()
    win_copies = [local(w3.at[i], wi.at[i], L_WIN + i) for i in range(3)]
    for cp in win_copies:
        cp.start()
    wo_copy = local(w_out, wo.at[own_j], L_WO)
    wo_copy.start()

    barrier = pltpu.get_barrier_semaphore()
    greet = [nxt, prv, other, partner, gate_to, gate_from] + y_peers + line_peers
    for to in greet:
        pl.semaphore_signal(barrier, inc=1, device_id=to, device_id_type=MESH)
    pl.semaphore_wait(barrier, len(greet))

    halo_copy = remote(tok.at[pl.ds(ROWS - HALO, HALO)], xo.at[1 - k, pl.ds(0, HALO)], S_HALO, nxt)
    halo_copy.start()
    row_a = pl.multiple_of((y * 4 + x) * 16, 16)
    row_b = pl.multiple_of(256 + (x * 4 + y) * 16, 16)
    wz = [
        remote(w_out.at[pl.ds(r, 16)], wo.at[own_j, pl.ds(r, 16)], S_WZ + i, partner)
        for i, r in enumerate((row_a, row_b))
    ]
    for cp in wz:
        cp.start()

    def norm_rows(first, count):
        def body(i, _):
            at = pl.ds(pl.multiple_of(first + i * 16, 16), 16)
            v = xo[k, at, :].astype(F32)
            scale = lax.rsqrt(jnp.mean(v * v, axis=1, keepdims=True) + 1e-6)
            xo[k, at, :] = (v * scale * gain[...].astype(F32)).astype(BF)
            return 0

        lax.fori_loop(0, count // 16, body, 0)

    xz, xd, xf = {}, {}, {}
    for c in ORDER:
        tok_copies[c].wait()
        if c == 0:
            halo_copy.wait_recv()

            @pl.when(order_at == 0)
            def _():
                xo[k, pl.ds(0, HALO), :] = jnp.zeros((HALO, WIDTH), BF)

        norm_rows(c * CROWS, CROWS)
        part = xo.at[k, pl.ds(c * CROWS, CROWS)]
        xz[c] = remote(part, xr.at[c, 1 - k], S_XZ + c, partner)
        xz[c].start()
        xd[c] = remote(part, part, S_XD + c, other)
        xd[c].start()
        xf[c] = remote(xr.at[c, k], xr.at[c, k], S_XF + c, other)

    for cp in wz:
        cp.wait_recv()
    wa, wbig = [], []
    for i in range(3):
        wa.append(remote(wo.at[far_j, pl.ds(row_a, 16)], wo.at[far_j, pl.ds(row_a, 16)], S_WA + i, x_peers[i]))
        wa.append(remote(wo.at[far_j, pl.ds(row_b, 16)], wo.at[far_j, pl.ds(row_b, 16)], S_WA + 3 + i, y_peers[i]))
    for cp in wa:
        cp.start()

    rate = decay[...]
    weight = resid[...] * jnp.sqrt(2.0 * rate)
    fall = jnp.exp(-rate)
    tap_rows = taps[...].astype(F32)
    for g in range(LG):
        cols = slice(g * 128, (g + 1) * 128)
        lam[g] = rate[:, cols]
        bb[g] = jnp.broadcast_to(bias[:, cols], (8, 128))
        for r in range(MODES):
            lb[g, r] = jnp.broadcast_to(rate[r : r + 1, cols], (8, 128))
            ab[g, r] = jnp.broadcast_to(fall[r : r + 1, cols], (8, 128))
            wb[g, r] = jnp.broadcast_to(weight[r : r + 1, cols], (8, 128))
        for j in range(TAPS):
            for i in range(3):
                tapb[g, j, i] = jnp.broadcast_to(tap_rows[i, j : j + 1, cols], (8, 128))

    def project_own(slot):
        def body(n, _):
            i = lax.div(n, 2)
            cols = pl.ds(pl.multiple_of(lax.rem(n, 2) * 256, 256), 256)
            v = jnp.dot(xo[slot], wi[i, :, cols], preferred_element_type=F32)
            proj[slot * 12 + 2 * n] = v[:, :128]
            proj[slot * 12 + 2 * n + 1] = v[:, 128:]
            return 0

        lax.fori_loop(0, 6, body, 0)

    def project_far(c):
        rows = pl.ds(c * CROWS, CROWS)

        def body(n, _):
            i = lax.div(n, 2)
            cols = pl.ds(pl.multiple_of(lax.rem(n, 2) * 256, 256), 256)
            lhs = xr[c].reshape(2 * CROWS, WIDTH)
            v = jnp.dot(lhs, wi[i, :, cols], preferred_element_type=F32)
            for a in range(2):
                for b in range(2):
                    proj[(2 + a) * 12 + 2 * n + b, rows] = v[a * CROWS : (a + 1) * CROWS, b * 128 : (b + 1) * 128]
            return 0

        lax.fori_loop(0, 6, body, 0)

    def spread(i):
        return pl.ds(HALO + i, PIECES, stride=STEPS)

    def fir(slot, g):
        base = slot * 12 + g
        weights = [tapb[g, j] for j in range(TAPS)]

        def row(at):
            return jnp.stack([proj[base + 4 * i, at, :] for i in range(3)])

        def body(n, past):
            past = list(past)
            for u in range(UNROLL):
                at = spread(n * UNROLL + u)
                now = row(at)
                total = weights[0] * now
                for j in range(1, TAPS):
                    total = total + weights[j] * past[-j]
                past = past[1:] + [now]
                proj[base, at, :] = total[0]
                proj[base + 4, at, :] = total[1] * total[2]
            return tuple(past)

        past = tuple(row(spread(m - (TAPS - 1))) for m in range(TAPS - 1))
        lax.fori_loop(0, STEPS // UNROLL, body, past)

    lane8 = lax.broadcasted_iota(jnp.int32, (1, 8, 128), 1)

    def scan(slot, g):
        base = slot * 12 + g

        def body(n, state):
            for u in range(UNROLL):
                at = spread(n * UNROLL + u)
                v = proj[base + 4, at, :]
                state = ab[g] * state + v[None]
                proj[base + 8, at, :] = jnp.sum(wb[g] * state, axis=0) + bb[g] * v
            return state

        v = lax.fori_loop(0, STEPS // UNROLL, body, jnp.zeros((MODES, 8, 128), F32))
        step = jnp.exp(lb[g] * float(-STEPS))
        for d in (1, 2, 4):
            back = pltpu.roll(v, d, 1)
            v = v + jnp.where(lane8 >= d, step * back, 0.0)
            step = step * step
        xe[slot * LG + g] = jnp.where(lane8 >= 1, pltpu.roll(v, 1, 1), 0.0)
        for r in range(MODES):
            et[slot, g, pl.ds(r, 1), :] = v[r, 7:8, :]

    def filter_slot(slot):
        def body(g, _):
            fir(slot, g)
            scan(slot, g)
            return 0

        lax.fori_loop(0, LG, body, 0)

    for cp in win_copies:
        cp.wait()
    project_own(k)
    xz[1].wait_recv()
    xf[1].start()
    wbig = []
    for cp in wa:
        cp.wait_recv()
    line_a = pl.ds(pl.multiple_of(y * 64, 64), 64)
    line_b = pl.ds(pl.multiple_of(256 + x * 64, 64), 64)
    for i in range(3):
        wbig.append(remote(wo.at[far_j, line_a], wo.at[far_j, line_a], S_WB + i, y_peers[i]))
        wbig.append(remote(wo.at[far_j, line_b], wo.at[far_j, line_b], S_WB + 3 + i, x_peers[i]))
    for cp in wbig:
        cp.start()
    for c in ORDER:
        xd[c].wait_recv()
    project_own(1 - k)
    wd = remote(w_out, wo.at[own_j], S_WD, other)
    wd.start()
    filter_slot(k)
    xz[0].wait_recv()
    xf[0].start()
    filter_slot(1 - k)
    xf[1].wait_recv()
    project_far(1)
    xf[0].wait_recv()
    project_far(0)
    wc = remote(wo.at[far_j], wo.at[far_j], S_WC, other)
    for c in ORDER[2:]:
        xz[c].wait_recv()
        xf[c].start()
        if c == ORDER[-1]:
            for cp in wbig:
                cp.wait_recv()
            wc.start()
        xf[c].wait_recv()
        project_far(c)

    filter_slot(2)
    filter_slot(3)

    def power(n):
        return jnp.exp(lam[...] * (-float(ROWS) * n.astype(F32)))

    lam3 = lam[...]
    one = jnp.exp(lam3 * -float(ROWS))
    m0, m1, m2, sg = 2 * p, 1 - p, 3 - 2 * p, 2 + p
    r1[line_at, 0] = (et[m2] + one * (et[m1] + one * et[m0])).astype(STATE)
    r1[line_at, 1] = et[sg].astype(STATE)
    e1 = [remote(r1.at[line_at], r1.at[line_at], S_E1 + i, line_peers[i]) for i in range(7)]
    for cp in e1:
        cp.start()
    cm, cq = power(1 - p), power(3 * p)
    group = jnp.exp(lam3 * -float(4 * ROWS))
    line = jnp.exp(lam3 * -float(16 * ROWS))
    for cp in e1:
        cp.wait_recv()
    before, totals = [], []
    for hh in range(2):
        run = jnp.zeros((LG, MODES, 128), F32)
        pre = run
        for xx in range(4):
            pre = jnp.where(x == xx, run, pre)
            run = group * run + cm * r1[hh * 4 + xx, 0].astype(F32) + cq * r1[(1 - hh) * 4 + xx, 1].astype(F32)
        before.append(pre)
        r2[y, hh] = run.astype(STATE)
    e2 = [remote(r2.at[y], r2.at[y], S_E2 + i, y_peers[i]) for i in range(3)]
    for cp in e2:
        cp.start()
    to_x = power(4 * x)
    to_y = power(16 * y)
    for cp in e2:
        cp.wait_recv()
    into = []
    plane = None
    for hh in range(2):
        run = jnp.zeros((LG, MODES, 128), F32)
        pre = run
        for yy in range(4):
            pre = jnp.where(y == yy, run, pre)
            run = line * run + r2[yy, hh].astype(F32)
        if hh == 1:
            pre = pre + to_y * plane
        plane = run
        into.append(to_x * pre + before[hh])
    mine = jnp.where(h == 0, into[0], into[1])
    theirs = jnp.where(h == 0, into[1], into[0])
    far_at = lax.rem(line_at + 4, 8)
    pf = p.astype(F32)
    s_main = power(p) * mine + pf * r1[far_at, 1].astype(F32)
    s_single = power(3 * (1 - p)) * theirs + (1.0 - pf) * r1[far_at, 0].astype(F32)
    sin[m0] = s_main
    s_main = one * s_main + et[m0]
    sin[m1] = s_main
    sin[m2] = one * s_main + et[m1]
    sin[sg] = s_single

    piece = lax.broadcasted_iota(jnp.int32, (1, 8, 128), 1).astype(F32) * float(-STEPS)

    def finish(slot, dst):
        def per_group(g, _):
            base = slot * 12 + g
            came = jnp.stack([jnp.broadcast_to(sin[slot, g, pl.ds(r, 1), :], (8, 128)) for r in range(MODES)])
            state = wb[g] * (xe[slot * LG + g] + jnp.exp(lb[g] * piece) * came)

            def body(n, state):
                for u in range(UNROLL):
                    at = spread(n * UNROLL + u)
                    state = ab[g] * state
                    v = proj[base + 8, at, :] + jnp.sum(state, axis=0)
                    proj[base + 8, at, :] = proj[base, at, :] * v
                return state

            lax.fori_loop(0, STEPS // UNROLL, body, state)
            return 0

        lax.fori_loop(0, LG, per_group, 0)
        for g in range(LG):
            dst[:, pl.ds(g * 128, 128)] = proj[slot * 12 + 8 + g, pl.ds(HALO, ROWS), :].astype(BF)

    sends = []
    for i, (slot, to) in enumerate(((2 + k, partner), (3 - k, gate_to), (1 - k, other))):
        finish(slot, gs.at[i])
        cp = remote(gs.at[i], gg.at[own_j], S_G + i, to)
        cp.start()
        sends.append(cp)
    for c in ORDER:
        xz[c].wait_send()
        xd[c].wait_send()
    res_copy = local(tok, xo.at[k, pl.ds(HALO, ROWS)], L_RES)
    res_copy.start()
    finish(k, gg.at[own_j])

    wo_copy.wait()
    res_copy.wait()

    def out_pass(js, kind):
        def body(n, _):
            cols = pl.ds(pl.multiple_of(n * OUT_COLS, OUT_COLS), OUT_COLS)
            tiles = OUT_COLS // 128
            if kind == 0:
                v = xo[k, pl.ds(HALO, ROWS), cols].astype(F32)
            else:
                v = jnp.concatenate([proj[n * tiles + i, pl.ds(0, ROWS), :] for i in range(tiles)], axis=1)
            for j in js:
                v = v + jnp.dot(gg[j], wo[j, :, cols], preferred_element_type=F32)
            if kind == 2:
                xo[1 - k, pl.ds(0, ROWS), cols] = v.astype(BF)
                local(xo.at[1 - k, pl.ds(0, ROWS), cols], out.at[:, cols], L_OUT + n).start()
            else:
                for i in range(tiles):
                    proj[n * tiles + i, pl.ds(0, ROWS), :] = v[:, i * 128 : (i + 1) * 128]
            return 0

        lax.fori_loop(0, OUT_TILES, body, 0)

    wd.wait_recv()
    sends[2].wait_recv()
    out_pass((own_j, oth_j), 0)
    wc.wait_recv()
    sends[0].wait_recv()
    out_pass((far_j,), 1)
    sends[1].wait_recv()
    out_pass((far2_j,), 2)

    for cp in [halo_copy] + wz + wa + wbig + [wd, wc] + list(xf.values()) + e1 + e2 + sends:
        cp.wait_send()
    for n in range(OUT_TILES):
        cols = pl.ds(n * OUT_COLS, OUT_COLS)
        local(xo.at[1 - k, pl.ds(0, ROWS), cols], out.at[:, cols], L_OUT + n).wait()


def shards(tokens, norm_gain, w_in, short_weight, conv_bias, decay_rates, residues, w_out):
    vmem = pl.BlockSpec(memory_space=pltpu.VMEM)
    hbm = pl.BlockSpec(memory_space=pl.ANY)
    return pl.pallas_call(
        kernel,
        out_shape=jax.ShapeDtypeStruct((ROWS, WIDTH), BF),
        in_specs=[hbm, vmem, hbm, vmem, vmem, vmem, vmem, hbm],
        out_specs=hbm,
        scratch_shapes=[
            pltpu.VMEM((2, SLOT, WIDTH), BF),
            pltpu.VMEM((CHUNKS, 2, CROWS, WIDTH), BF),
            pltpu.VMEM((3, WIDTH, CH), BF),
            pltpu.VMEM((4, CH, WIDTH), BF),
            pltpu.VMEM((48, SLOT, 128), F32),
            pltpu.VMEM((3, ROWS, CH), BF),
            pltpu.VMEM((4, ROWS, CH), BF),
            pltpu.VMEM((LG, TAPS, 3, 8, 128), F32),
            pltpu.VMEM((LG, MODES, 8, 128), F32),
            pltpu.VMEM((LG, MODES, 8, 128), F32),
            pltpu.VMEM((LG, MODES, 8, 128), F32),
            pltpu.VMEM((LG, 8, 128), F32),
            pltpu.VMEM((LG, MODES, 128), F32),
            pltpu.VMEM((4 * LG, MODES, 8, 128), F32),
            pltpu.VMEM((4, LG, MODES, 128), F32),
            pltpu.VMEM((4, LG, MODES, 128), F32),
            pltpu.VMEM((8, 2, LG, MODES, 128), STATE),
            pltpu.VMEM((4, 2, LG, MODES, 128), STATE),
            pltpu.SemaphoreType.DMA((S_N,)),
            pltpu.SemaphoreType.DMA((S_N,)),
            pltpu.SemaphoreType.DMA((L_N,)),
        ],
        compiler_params=pltpu.CompilerParams(
            collective_id=0, has_side_effects=True, vmem_limit_bytes=60 * 2**20
        ),
        cost_estimate=pl.CostEstimate(flops=26 * 10**9, bytes_accessed=25 * 2**20, transcendentals=0),
    )(
        tokens,
        norm_gain.reshape(1, WIDTH),
        w_in.transpose(1, 0, 2),
        short_weight.transpose(1, 0, 2),
        conv_bias.reshape(1, CH),
        decay_rates,
        residues,
        w_out,
    )


def solution(mesh):
    in_specs = (
        P(("ctx", "tp"), None),
        P(),
        P(None, None, "tp"),
        P(None, None, "tp"),
        P("tp"),
        P(None, "tp"),
        P(None, "tp"),
        P("tp", None),
    )
    return jax.shard_map(
        shards, mesh=mesh, in_specs=in_specs, out_specs=P(("ctx", "tp"), None), check_vma=False
    )
```

time: 578 us -> 109 us (0.19); the launches traced: 569 us -> 109 us
  waiting for transfers between devices: 292 us -> 0 us
  matrix products: 104 us -> 0 us
  Pallas kernels: 0 us -> 104 us
  other arithmetic: 65.4 us -> 0 us
  local copies, waits for them, and re-layouts: 50.3 us -> 5.22 us
  blocking collectives: 33.7 us -> 0 us
  between operations: 14 us -> 0.01 us
  starting transfers between devices: 9.57 us -> 0 us
    reduce_scatter x1 -> x0, waiting for transfers between devices: 116 us -> none  [shards(): lax.psum_scatter(lax.optimization_barrier(partial_value.astype(jnp.bfloat...]
    pallas_call x0 -> x1, Pallas kernels: none -> 104 us  [shards(): pl.pallas_call(kernel, out_shape=jax.ShapeDtypeStruct((ROWS, WIDTH), BF),...]
    dot_general x7 -> x0, matrix products: 104 us -> none  [the longest x1 33.8 us: long_filter(): jnp.einsum('crnm,crm->crn', carried, block_ends, precision=highest_precis...]
    all_gather x1 -> x0, waiting for transfers between devices: 103 us -> none  [shards(): lax.all_gather(normed, 'tp', axis=0, tiled=True)]
    all_to_all x1 -> x0, waiting for transfers between devices: 72.7 us -> none  [shards(): lax.all_to_all(streams, 'ctx', split_axis=1, concat_axis=2, tiled=True)]
    add x2 -> x0, other arithmetic: 35.3 us -> none  [the longest x1 35.3 us: short_filter(): summed + tap_weights[tap_index].astype(jnp.float32)[:, :, None] * padded[...]
    all_to_all x1 -> x0, blocking collectives: 33.7 us -> none  [shards(): lax.all_to_all(returned, 'ctx', split_axis=1, concat_axis=0, tiled=True)]
    convert_element_type x8 -> x0, other arithmetic: 26.3 us -> none  [the longest x1 9.28 us: shards(): moved.astype(jnp.float32)]
  transfers between devices with their start and end apart: 3 -> 0, of which waited for: 3 -> 0; matrix products, arithmetic and copies ran while one was open for 7% -> 0% of each run, Pallas kernels for 0% -> 0%
where the time goes in v1:
time: 109 us
  Pallas kernels  104 us (95%)
  local copies, waits for them, and re-layouts  5.22 us (5%)
    pallas_call x1, Pallas kernels, shards(): pl.pallas_call(kernel, out_shape=jax.ShapeDtypeStruct((ROWS, WIDTH), BF),...  104 us
    unnamed x1, local copies, waits for them, and re-layouts  3.91 us

profile of v1, /device:TPU:1, one launch (start us, length us, event | category | flops | bytes accessed | tf_op | source)
XLA Modules:
  0.0 109.1 jit_solution(13992570613282674202)
XLA Ops:
  0.0 1.3 %reshape.6.gain = bf16[1,4096]{1,0:T(2,128)(2,1)} reshape(bf16[4096]{0:T(1024)(128)(2,1)} %param.9) | data formatting | bytes 16384 | tf_op jit(solution)/shard_map/reshape | solution.py:474
  1.3 103.9 %shard_map.82 = bf16[384,4096]{1,0:T(8,128)(2,1)} custom-call(bf16[384,4096]{1,0:T(8,128)(2,1)} %tok.1, bf16[1,4096]{1,0:T(2,128)(2,1)} %reshape.6.gain, bf16[3,4096,512]{2,1,0:T(8,128)(2,1)} %bitcast.3, bf16[3,7,512]{2,1,0:T(8,128)(2,1)} %bitcast.4, f32[1,512]{1,0:T(1,128)} %bitcast.5, f32[16,512]{1,0:T(8,128)} %decay.1, f32[16,512]{1,0:T(8,128)} %resid.1, ...), custom_call_target="tpu_custom_call" | custom-call | flops 25999998976 | bytes 26214400 | tf_op jit(solution)/shard_map/pallas_call | solution.py:440
  105.2 3.9 %copy.10 = bf16[384,4096]{1,0:T(8,128)(2,1)} copy(bf16[384,4096]{1,0:T(8,128)(2,1)} %shard_map.82) | data formatting | bytes 6291456

commit v2 on v1

v2 whole, which is shorter than its diff:
```python
import functools

import jax
import jax.numpy as jnp
from jax import lax
from jax.experimental import pallas as pl
from jax.experimental.pallas import tpu as pltpu
from jax.sharding import PartitionSpec as P

MESH = pl.DeviceIdType.MESH
BF, F32 = jnp.bfloat16, jnp.float32
STATE = F32

ROWS = 384
HALO = 16
SLOT = ROWS + HALO
WIDTH = 4096
CH = 512
FIRST = (0, 112, 208, 304)
COUNT = (112, 96, 96, 96)
CHUNKS = 4
ORDER = (1, 0, 2, 3)
PARTS = ((0, 0, 112), (1, 0, 96), (2, 0, 96), (3, 0, 48), (3, 48, 48))
LATE = 96
EARLY = ROWS - LATE
PIECES = 8
MODES = 16
TAPS = 7
LG = CH // 128
UNROLL = 12

S_HALO = 0
S_XZ = 1
S_XD = S_XZ + len(PARTS)
S_XF = S_XD + len(PARTS)
S_WZ = S_XF + len(PARTS)
S_WD = S_WZ + 2
S_WA = S_WD + 1
S_WB = S_WA + 6
S_WC = S_WB + 6
S_EZ = S_WC + 1
S_EX = S_EZ + LG
S_EY = S_EX + 3 * LG
S_G = S_EY + 3 * LG
S_N = S_G + 3 * LG
L_TOK = 0
L_WIN = CHUNKS
L_WO = L_WIN + 3
L_RES = L_WO + 1
L_OUT = L_RES + 1
OUT_TILES = 4
L_N = L_OUT + OUT_TILES
OUT_COLS = WIDTH // OUT_TILES


def kernel(
    tok, gain, w3, taps, bias, decay, resid, w_out, out,
    xo, xr, wi, wo, proj, late, gs, gg, tapb, ab, wb, lb, bb, lam, xe, et, ea, sin, grow, bf, mq, rz, r1, r2, ss, rs, ls,
):
    ctx = lax.axis_index("ctx")
    tp = lax.axis_index("tp")
    x = lax.rem(ctx, 4)
    y = lax.rem(lax.div(ctx, 4), 4)
    h = lax.div(ctx, 16)
    p = lax.div(tp, 2)
    k = lax.rem(tp, 2)
    z = 2 * h + p
    s = 2 * k - 1

    def dev(dx, dy, dz, core):
        zz = lax.rem(dz + 4, 4)
        return (lax.div(zz, 2) * 16 + lax.rem(dy, 4) * 4 + lax.rem(dx, 4), lax.rem(zz, 2) * 2 + core)

    order_at = ctx * 4 + tp
    nxt = lax.rem(order_at + 1, 128)
    prv = lax.rem(order_at + 127, 128)
    nxt = (lax.div(nxt, 4), lax.rem(nxt, 4))
    prv = (lax.div(prv, 4), lax.rem(prv, 4))
    other = dev(x, y, z, 1 - k)
    partner = dev(x, y, z + s, 1 - k)
    gate_to = dev(x, y, z - s, k)
    gate_from = dev(x, y, z + s, k)
    x_peers = [dev(x + d, y, z, k) for d in (1, 2, 3)]
    y_peers = [dev(x, y + d, z, k) for d in (1, 2, 3)]
    mirror = dev(x, y, z + 2, k)
    own_j = 2 * p + k
    oth_j = 2 * p + 1 - k
    far_j = 2 * (1 - p) + 1 - k
    far2_j = 2 * (1 - p) + k

    def remote(src, dst, at, to):
        return pltpu.make_async_remote_copy(
            src_ref=src, dst_ref=dst, send_sem=ss.at[at], recv_sem=rs.at[at], device_id=to, device_id_type=MESH
        )

    def local(src, dst, at):
        return pltpu.make_async_copy(src, dst, ls.at[at])

    tok_copies = {}
    for c in ORDER:
        to = max(FIRST[c], HALO)
        count = FIRST[c] + COUNT[c] - to
        tok_copies[c] = local(tok.at[pl.ds(to - HALO, count)], xo.at[k, pl.ds(to, count)], L_TOK + c)
        tok_copies[c].start()
    win_copies = [local(w3.at[i], wi.at[i], L_WIN + i) for i in range(3)]
    for cp in win_copies:
        cp.start()
    wo_copy = local(w_out, wo.at[own_j], L_WO)

    barrier = pltpu.get_barrier_semaphore()
    greet = [nxt, prv, other, partner, gate_to, gate_from, mirror] + x_peers + y_peers
    for to in greet:
        pl.semaphore_signal(barrier, inc=1, device_id=to, device_id_type=MESH)
    pl.semaphore_wait(barrier, len(greet))

    halo_copy = remote(tok.at[pl.ds(ROWS - HALO, HALO)], xo.at[1 - k, pl.ds(0, HALO)], S_HALO, nxt)
    halo_copy.start()
    row_a = pl.multiple_of((y * 4 + x) * 16, 16)
    row_b = pl.multiple_of(256 + (x * 4 + y) * 16, 16)
    wz = [
        remote(w_out.at[pl.ds(r, 16)], wo.at[own_j, pl.ds(r, 16)], S_WZ + i, partner)
        for i, r in enumerate((row_a, row_b))
    ]
    for cp in wz:
        cp.start()

    for i in range(WIDTH // 128):
        grow[:, i * 128 : (i + 1) * 128] = gain[i : i + 1, :].astype(F32)

    def norm_rows(first, count):
        def body(i, _):
            at = pl.ds(pl.multiple_of(first + i * 16, 16), 16)
            v = xo[k, at, :].astype(F32)
            total = v[:, :128] * v[:, :128]
            for n in range(1, WIDTH // 128):
                total = total + v[:, n * 128 : (n + 1) * 128] * v[:, n * 128 : (n + 1) * 128]
            scale = lax.rsqrt(jnp.sum(total, axis=1, keepdims=True) * (1.0 / WIDTH) + 1e-6)
            xo[k, at, :] = (v * scale * grow[...]).astype(BF)
            return 0

        lax.fori_loop(0, count // 16, body, 0)

    xz, xd, xf = {}, {}, {}
    for c in ORDER:
        tok_copies[c].wait()
        if c == 0:
            halo_copy.wait_recv()

            @pl.when(order_at == 0)
            def _():
                xo[k, pl.ds(0, HALO), :] = jnp.zeros((HALO, WIDTH), BF)

        norm_rows(FIRST[c], COUNT[c])
        for at, (chunk, off, count) in enumerate(PARTS):
            if chunk != c:
                continue

            def landed(core):
                row = 2 * FIRST[c] + core * COUNT[c] + off
                return xr.at[pl.ds(pl.multiple_of(row, 16), count)]

            part = xo.at[k, pl.ds(FIRST[c] + off, count)]
            xz[at] = remote(part, landed(1 - k), S_XZ + at, partner)
            xz[at].start()
            xd[at] = remote(part, part, S_XD + at, other)
            xd[at].start()
            xf[at] = remote(landed(k), landed(k), S_XF + at, other)

    for cp in wz:
        cp.wait_recv()
    wa, wbig = [], []
    for i in range(3):
        wa.append(remote(wo.at[far_j, pl.ds(row_a, 16)], wo.at[far_j, pl.ds(row_a, 16)], S_WA + i, x_peers[i]))
        wa.append(remote(wo.at[far_j, pl.ds(row_b, 16)], wo.at[far_j, pl.ds(row_b, 16)], S_WA + 3 + i, y_peers[i]))
    for cp in wa:
        cp.start()

    rate = decay[...]
    weight = resid[...] * jnp.sqrt(2.0 * rate)
    fall = jnp.exp(-rate)
    tap_rows = taps[...].astype(F32)
    for g in range(LG):
        cols = slice(g * 128, (g + 1) * 128)
        lam[g] = rate[:, cols]
        bb[g] = jnp.broadcast_to(bias[:, cols], (8, 128))
        for r in range(MODES):
            lb[g, r] = jnp.broadcast_to(rate[r : r + 1, cols], (8, 128))
            ab[g, r] = jnp.broadcast_to(fall[r : r + 1, cols], (8, 128))
            wb[g, r] = jnp.broadcast_to(weight[r : r + 1, cols], (8, 128))
        for j in range(TAPS):
            for i in range(3):
                tapb[g, j, i] = jnp.broadcast_to(tap_rows[i, j : j + 1, cols], (8, 128))

    def project_own(slot):
        def body(n, _):
            v = jnp.dot(xo[slot], wi[n], preferred_element_type=F32)
            for b in range(4):
                proj[slot * 12 + 4 * n + b] = v[:, b * 128 : (b + 1) * 128]
            return 0

        lax.fori_loop(0, 3, body, 0, unroll=3)

    def project_far(c):
        first, count = FIRST[c], COUNT[c]

        def body(n, _):
            v = jnp.dot(xr[pl.ds(2 * first, 2 * count)], wi[n], preferred_element_type=F32)
            for a in range(2):
                for b in range(4):
                    part = v[a * count : (a + 1) * count, b * 128 : (b + 1) * 128]
                    if c < CHUNKS - 1:
                        proj[(2 + a) * 12 + 4 * n + b, pl.ds(first, count)] = part
                    else:
                        late[a * 12 + 4 * n + b, pl.ds(HALO, LATE)] = part
                    if c == CHUNKS - 2:
                        late[a * 12 + 4 * n + b, pl.ds(0, HALO)] = part[count - HALO :]
            return 0

        lax.fori_loop(0, 3, body, 0)

    def spread(steps, i):
        return pl.ds(HALO + i, PIECES, stride=steps)

    def fir(ref, base, steps, g, streams):
        base = base + g

        def body(n, past):
            places = [spread(steps, n * UNROLL + u) for u in range(UNROLL)]
            fresh = [[ref[base + 4 * i, at, :] for at in places] for i in streams]
            rows = [list(old) + new for old, new in zip(past, fresh)]
            totals = []
            for i, row in zip(streams, rows):
                stream = []
                for u in range(UNROLL):
                    t = [tapb[g, j, i] * row[u + TAPS - 1 - j] for j in range(TAPS)]
                    stream.append(((t[0] + t[1]) + (t[2] + t[3])) + ((t[4] + t[5]) + t[6]))
                totals.append(stream)
            for u, at in enumerate(places):
                if streams == (0,):
                    ref[base, at, :] = totals[0][u]
                else:
                    ref[base + 4, at, :] = totals[0][u] * totals[1][u]
            return tuple(tuple(row[UNROLL:]) for row in rows)

        past = tuple(
            tuple(ref[base + 4 * i, spread(steps, m - (TAPS - 1)), :] for m in range(TAPS - 1)) for i in streams
        )
        lax.fori_loop(0, steps // UNROLL, body, past)

    lane8 = lax.broadcasted_iota(jnp.int32, (1, 8, 128), 1)

    def mode_sum(v):
        count = MODES
        while count > 1:
            count //= 2
            v = v[:count] + v[count:]
        return v[0]

    def scan(ref, base, steps, unit, g, outputs, ends):
        base = base + g

        def body(n, state):
            places = [spread(steps, n * UNROLL + u) for u in range(UNROLL)]
            values = [ref[base + 4, at, :] for at in places]
            sums = []
            for v in values:
                state = ab[g] * state + v[None]
                if outputs:
                    sums.append(mode_sum(wb[g] * state) + bb[g] * v)
            for at, v in zip(places, sums):
                ref[base + 8, at, :] = v
            return state

        v = lax.fori_loop(0, steps // UNROLL, body, jnp.zeros((MODES, 8, 128), F32))
        if not ends:
            return
        step = jnp.exp(lb[g] * float(-steps))
        for d in (1, 2, 4):
            back = pltpu.roll(v, d, 1)
            v = v + jnp.where(lane8 >= d, step * back, 0.0)
            step = step * step
        xe[unit * LG + g] = jnp.where(lane8 >= 1, pltpu.roll(v, 1, 1), 0.0)
        for r in range(MODES):
            et[unit, g, pl.ds(r, 1), :] = v[r, 7:8, :]

    def filter_own(slot):
        def body(g, _):
            fir(proj, slot * 12, ROWS // PIECES, g, (1, 2))
            scan(proj, slot * 12, ROWS // PIECES, slot, g, True, True)
            fir(proj, slot * 12, ROWS // PIECES, g, (0,))
            return 0

        lax.fori_loop(0, LG, body, 0)

    def filter_early():
        def body(n, _):
            i, g = lax.div(n, LG), lax.rem(n, LG)
            fir(proj, 24 + i * 12, EARLY // PIECES, g, (1, 2))
            scan(proj, 24 + i * 12, EARLY // PIECES, 2 + i, g, False, True)
            return 0

        lax.fori_loop(0, 2 * LG, body, 0)

    def filter_late(g):
        for i in range(2):
            fir(late, i * 12, LATE // PIECES, g, (1, 2))
            scan(late, i * 12, LATE // PIECES, 4 + i, g, False, True)

    def filter_rest(g):
        def body(i, _):
            fir(proj, 24 + i * 12, EARLY // PIECES, g, (0,))
            scan(proj, 24 + i * 12, EARLY // PIECES, 0, g, True, False)
            fir(late, i * 12, LATE // PIECES, g, (0,))
            scan(late, i * 12, LATE // PIECES, 0, g, True, False)
            return 0

        lax.fori_loop(0, 2, body, 0)

    for cp in win_copies:
        cp.wait()
    wo_copy.start()
    project_own(k)
    xz[1].wait_recv()
    xf[1].start()
    wbig = []
    for cp in wa:
        cp.wait_recv()
    line_a = pl.ds(pl.multiple_of(y * 64, 64), 64)
    line_b = pl.ds(pl.multiple_of(256 + x * 64, 64), 64)
    for i in range(3):
        wbig.append(remote(wo.at[far_j, line_a], wo.at[far_j, line_a], S_WB + i, y_peers[i]))
        wbig.append(remote(wo.at[far_j, line_b], wo.at[far_j, line_b], S_WB + 3 + i, x_peers[i]))
    for cp in wbig:
        cp.start()
    for at in xd:
        xd[at].wait_recv()
    project_own(1 - k)
    wd = remote(w_out, wo.at[own_j], S_WD, other)
    wd.start()
    xf[1].wait_recv()
    project_far(1)
    filter_own(k)
    xz[0].wait_recv()
    xf[0].start()
    xf[0].wait_recv()
    project_far(0)
    filter_own(1 - k)
    xz[2].wait_recv()
    xf[2].start()
    xf[2].wait_recv()
    project_far(2)
    filter_early()
    wc = remote(wo.at[far_j], wo.at[far_j], S_WC, other)
    for at in (3, 4):
        xz[at].wait_recv()
        xf[at].start()
    for at in (3, 4):
        xf[at].wait_recv()
    project_far(3)

    m0, m1, m2, sg = 2 * p, 1 - p, 3 - 2 * p, 2 + p
    ez, ex, ey, sends = {}, {}, {}, {}

    def power(g, n):
        return jnp.exp(lam[g] * (-float(ROWS) * jnp.asarray(n).astype(F32)))

    def fall_over(g, tokens):
        return jnp.exp(lam[g] * -float(tokens))

    def send_z(g):
        one = power(g, 1)
        for i in range(2):
            ea[i, g] = et[2 + i, g]
            et[2 + i, g] = fall_over(g, LATE) * et[2 + i, g] + et[4 + i, g]
        mq[g, 0] = (et[m2, g] + one * (et[m1, g] + one * et[m0, g])).astype(STATE)
        mq[g, 1] = et[sg, g].astype(STATE)
        ez[g] = remote(mq.at[g], rz.at[g], S_EZ + g, mirror)
        ez[g].start()

    def send_x(g):
        cm, cq = power(g, 1 - p), power(g, 3 * p)
        ez[g].wait_recv()
        own, far = mq[g].astype(F32), rz[g].astype(F32)
        r1[g, x, h] = (cm * own[0] + cq * far[1]).astype(STATE)
        r1[g, x, 1 - h] = (cm * far[0] + cq * own[1]).astype(STATE)
        ex[g] = [remote(r1.at[g, x], r1.at[g, x], S_EX + 3 * g + i, x_peers[i]) for i in range(3)]
        for cp in ex[g]:
            cp.start()

    def send_y(g):
        group = power(g, 4)
        for cp in ex[g]:
            cp.wait_recv()
        for hh in range(2):
            run = jnp.zeros((MODES, 128), F32)
            pre = run
            for xx in range(4):
                pre = jnp.where(x == xx, run, pre)
                run = group * run + r1[g, xx, hh].astype(F32)
            bf[g, hh] = pre
            r2[g, y, hh] = run.astype(STATE)
        ey[g] = [remote(r2.at[g, y], r2.at[g, y], S_EY + 3 * g + i, y_peers[i]) for i in range(3)]
        for cp in ey[g]:
            cp.start()

    def states(g):
        line = power(g, 16)
        to_x = power(g, 4 * x)
        to_y = power(g, 16 * y)
        one = power(g, 1)
        for cp in ey[g]:
            cp.wait_recv()
        into = []
        plane = None
        for hh in range(2):
            run = jnp.zeros((MODES, 128), F32)
            pre = run
            for yy in range(4):
                pre = jnp.where(y == yy, run, pre)
                run = line * run + r2[g, yy, hh].astype(F32)
            if hh == 1:
                pre = pre + to_y * plane
            plane = run
            into.append(to_x * pre + bf[g, hh])
        mine = jnp.where(h == 0, into[0], into[1])
        theirs = jnp.where(h == 0, into[1], into[0])
        pf = p.astype(F32)
        s_main = power(g, p) * mine + pf * rz[g, 1].astype(F32)
        sin[sg, g] = power(g, 3 * (1 - p)) * theirs + (1.0 - pf) * rz[g, 0].astype(F32)
        sin[m0, g] = s_main
        s_main = one * s_main + et[m0, g]
        sin[m1, g] = s_main
        sin[m2, g] = one * s_main + et[m1, g]
        for i in range(2):
            sin[4 + i, g] = fall_over(g, EARLY) * sin[2 + i, g] + ea[i, g]

    piece = lax.broadcasted_iota(jnp.int32, (1, 8, 128), 1).astype(F32)

    def finish_part(ref, base, steps, unit, g, dst, first):
        base = base + g
        came = jnp.stack([jnp.broadcast_to(sin[unit, g, pl.ds(r, 1), :], (8, 128)) for r in range(MODES)])
        state = wb[g] * (xe[unit * LG + g] + jnp.exp(lb[g] * piece * float(-steps)) * came)

        def body(n, state):
            places = [spread(steps, n * UNROLL + u) for u in range(UNROLL)]
            values = [(ref[base, at, :], ref[base + 8, at, :]) for at in places]
            gated = []
            for q, v in values:
                state = ab[g] * state
                gated.append(q * (v + mode_sum(state)))
            for at, v in zip(places, gated):
                ref[base + 8, at, :] = v
            return state

        lax.fori_loop(0, steps // UNROLL, body, state)
        dst[pl.ds(first, PIECES * steps), :] = ref[base + 8, pl.ds(HALO, PIECES * steps), :].astype(BF)

    def finish(slot, g, dst, far):
        if far:
            finish_part(proj, slot * 12, EARLY // PIECES, slot, g, dst, 0)
            finish_part(late, (slot - 2) * 12, LATE // PIECES, slot + 2, g, dst, EARLY)
        else:
            finish_part(proj, slot * 12, ROWS // PIECES, slot, g, dst, 0)

    def finish_all(g):
        for i, (slot, to) in enumerate(((2 + k, partner), (3 - k, gate_to), (1 - k, other))):
            finish(slot, g, gs.at[i, g], i < 2)
            sends[i, g] = remote(gs.at[i, g], gg.at[own_j, g], S_G + 3 * g + i, to)
            sends[i, g].start()
        finish(k, g, gg.at[own_j, g], False)

    for g in range(LG):
        filter_late(g)
        send_z(g)
    for cp in wbig:
        cp.wait_recv()
    wc.start()
    filter_rest(0)
    for g in range(LG):
        send_x(g)
    filter_rest(1)
    for g in range(LG):
        send_y(g)
    filter_rest(2)
    states(0)
    finish_all(0)
    filter_rest(3)
    for at in xz:
        xz[at].wait_send()
        xd[at].wait_send()
    res_copy = local(tok, xo.at[k, pl.ds(HALO, ROWS)], L_RES)
    res_copy.start()
    for g in range(1, LG):
        states(g)
        finish_all(g)

    wo_copy.wait()
    res_copy.wait()

    def out_pass(js, halves, kind):
        def body(n, _):
            cols = pl.ds(pl.multiple_of(n * OUT_COLS, OUT_COLS), OUT_COLS)
            tiles = OUT_COLS // 128
            if kind == 0:
                v = xo[k, pl.ds(HALO, ROWS), cols].astype(F32)
            else:
                v = jnp.concatenate([proj[n * tiles + i, pl.ds(0, ROWS), :] for i in range(tiles)], axis=1)
            for j in js:
                for half in halves:
                    lhs = jnp.concatenate([gg[j, 2 * half], gg[j, 2 * half + 1]], axis=1)
                    rows = slice(half * 256, half * 256 + 256)
                    v = v + jnp.dot(lhs, wo[j, rows, cols], preferred_element_type=F32)
            if kind == 2:
                xo[1 - k, pl.ds(0, ROWS), cols] = v.astype(BF)
                local(xo.at[1 - k, pl.ds(0, ROWS), cols], out.at[:, cols], L_OUT + n).start()
            else:
                for i in range(tiles):
                    proj[n * tiles + i, pl.ds(0, ROWS), :] = v[:, i * 128 : (i + 1) * 128]
            return 0

        lax.fori_loop(0, OUT_TILES, body, 0)

    wd.wait_recv()
    for g in range(LG):
        sends[2, g].wait_recv()
    out_pass((own_j, oth_j), (0, 1), 0)
    wc.wait_recv()
    for half in (0, 1):
        for g in (2 * half, 2 * half + 1):
            for i in range(2):
                sends[i, g].wait_recv()
        out_pass((far_j, far2_j), (half,), 1 + half)

    for cp in [halo_copy] + wz + wa + wbig + [wd, wc] + list(xf.values()) + list(ez.values()) + list(sends.values()):
        cp.wait_send()
    for g in range(LG):
        for cp in ex[g] + ey[g]:
            cp.wait_send()
    for n in range(OUT_TILES):
        cols = pl.ds(n * OUT_COLS, OUT_COLS)
        local(xo.at[1 - k, pl.ds(0, ROWS), cols], out.at[:, cols], L_OUT + n).wait()


def shards(tokens, norm_gain, w_in, short_weight, conv_bias, decay_rates, residues, w_out):
    vmem = pl.BlockSpec(memory_space=pltpu.VMEM)
    hbm = pl.BlockSpec(memory_space=pl.ANY)
    return pl.pallas_call(
        kernel,
        out_shape=jax.ShapeDtypeStruct((ROWS, WIDTH), BF),
        in_specs=[hbm, vmem, hbm, vmem, vmem, vmem, vmem, hbm],
        out_specs=hbm,
        scratch_shapes=[
            pltpu.VMEM((2, SLOT, WIDTH), BF),
            pltpu.VMEM((2 * SLOT, WIDTH), BF),
            pltpu.VMEM((3, WIDTH, CH), BF),
            pltpu.VMEM((4, CH, WIDTH), BF),
            pltpu.VMEM((48, SLOT, 128), F32),
            pltpu.VMEM((24, HALO + LATE, 128), F32),
            pltpu.VMEM((3, LG, ROWS, 128), BF),
            pltpu.VMEM((4, LG, ROWS, 128), BF),
            pltpu.VMEM((LG, TAPS, 3, 8, 128), F32),
            pltpu.VMEM((LG, MODES, 8, 128), F32),
            pltpu.VMEM((LG, MODES, 8, 128), F32),
            pltpu.VMEM((LG, MODES, 8, 128), F32),
            pltpu.VMEM((LG, 8, 128), F32),
            pltpu.VMEM((LG, MODES, 128), F32),
            pltpu.VMEM((6 * LG, MODES, 8, 128), F32),
            pltpu.VMEM((6, LG, MODES, 128), F32),
            pltpu.VMEM((2, LG, MODES, 128), F32),
            pltpu.VMEM((6, LG, MODES, 128), F32),
            pltpu.VMEM((1, WIDTH), F32),
            pltpu.VMEM((LG, 2, MODES, 128), F32),
            pltpu.VMEM((LG, 2, MODES, 128), STATE),
            pltpu.VMEM((LG, 2, MODES, 128), STATE),
            pltpu.VMEM((LG, 4, 2, MODES, 128), STATE),
            pltpu.VMEM((LG, 4, 2, MODES, 128), STATE),
            pltpu.SemaphoreType.DMA((S_N,)),
            pltpu.SemaphoreType.DMA((S_N,)),
            pltpu.SemaphoreType.DMA((L_N,)),
        ],
        compiler_params=pltpu.CompilerParams(
            collective_id=0, has_side_effects=True, vmem_limit_bytes=60 * 2**20
        ),
        cost_estimate=pl.CostEstimate(flops=26 * 10**9, bytes_accessed=25 * 2**20, transcendentals=0),
    )(
        tokens,
        norm_gain.reshape(WIDTH // 128, 128),
        w_in.transpose(1, 0, 2),
        short_weight.transpose(1, 0, 2),
        conv_bias.reshape(1, CH),
        decay_rates,
        residues,
        w_out,
    )


def solution(mesh):
    in_specs = (
        P(("ctx", "tp"), None),
        P(),
        P(None, None, "tp"),
        P(None, None, "tp"),
        P("tp"),
        P(None, "tp"),
        P(None, "tp"),
        P("tp", None),
    )
    return jax.shard_map(
        shards, mesh=mesh, in_specs=in_specs, out_specs=P(("ctx", "tp"), None), check_vma=False
    )
```

time: 109 us -> 92 us (0.84)
  Pallas kernels: 104 us -> 87.9 us
  local copies, waits for them, and re-layouts: 5.22 us -> 3.91 us
    pallas_call x1, Pallas kernels: 104 us -> 87.9 us  [shards(): pl.pallas_call(kernel, out_shape=jax.ShapeDtypeStruct((ROWS, WIDTH), BF),...]
    reshape x1 -> x0, local copies, waits for them, and re-layouts: 1.31 us -> none  [shards(): norm_gain.reshape(1, WIDTH)]
where the time goes in v2:
time: 92 us; the launch traced here: 91.8 us
  Pallas kernels  87.9 us (96%)
  local copies, waits for them, and re-layouts  3.91 us (4%)
    pallas_call x1, Pallas kernels, shards(): pl.pallas_call(kernel, out_shape=jax.ShapeDtypeStruct((ROWS, WIDTH), BF),...  87.9 us
    unnamed x1, local copies, waits for them, and re-layouts  3.91 us

profile of v2, /device:TPU:1, one launch (start us, length us, event | category | flops | bytes accessed | tf_op | source)
XLA Modules:
  0.0 91.8 jit_solution(14922561028124235650)
XLA Ops:
  0.0 87.9 %shard_map.82 = bf16[384,4096]{1,0:T(8,128)(2,1)} custom-call(bf16[384,4096]{1,0:T(8,128)(2,1)} %tok.1, bf16[32,128]{1,0:T(8,128)(2,1)} %bitcast.6, bf16[3,4096,512]{2,1,0:T(8,128)(2,1)} %bitcast.4, bf16[3,7,512]{2,1,0:T(8,128)(2,1)} %bitcast.5, f32[1,512]{1,0:T(1,128)} %bitcast.7, f32[16,512]{1,0:T(8,128)} %decay.1, f32[16,512]{1,0:T(8,128)} %resid.1, ...), custom_call_target="tpu_custom_call" | custom-call | flops 25999998976 | bytes 26214400 | tf_op jit(solution)/shard_map/pallas_call | solution.py:547
  87.9 3.9 %copy.10 = bf16[384,4096]{1,0:T(8,128)(2,1)} copy(bf16[384,4096]{1,0:T(8,128)(2,1)} %shard_map.82) | data formatting | bytes 6291456

commit v3 on v2

--- a/solution.py
+++ b/solution.py
@@ -462,28 +462,30 @@
         else:
             finish_part(proj, slot * 12, ROWS // PIECES, slot, g, dst, 0)
 
-    def finish_all(g):
-        for i, (slot, to) in enumerate(((2 + k, partner), (3 - k, gate_to), (1 - k, other))):
-            finish(slot, g, gs.at[i, g], i < 2)
-            sends[i, g] = remote(gs.at[i, g], gg.at[own_j, g], S_G + 3 * g + i, to)
-            sends[i, g].start()
-        finish(k, g, gg.at[own_j, g], False)
+    def finish_send(i, slot, to, g):
+        finish(slot, g, gs.at[i, g], i < 2)
+        sends[i, g] = remote(gs.at[i, g], gg.at[own_j, g], S_G + 3 * g + i, to)
+        sends[i, g].start()
+
+    def finish_far(g):
+        finish_send(0, 2 + k, partner, g)
+        finish_send(1, 3 - k, gate_to, g)
 
     for g in range(LG):
         filter_late(g)
         send_z(g)
+    filter_rest(0)
+    for g in range(LG):
+        send_x(g)
+    filter_rest(1)
+    for g in range(LG):
+        send_y(g)
     for cp in wbig:
         cp.wait_recv()
     wc.start()
-    filter_rest(0)
-    for g in range(LG):
-        send_x(g)
-    filter_rest(1)
-    for g in range(LG):
-        send_y(g)
     filter_rest(2)
     states(0)
-    finish_all(0)
+    finish_far(0)
     filter_rest(3)
     for at in xz:
         xz[at].wait_send()
@@ -492,7 +494,11 @@
     res_copy.start()
     for g in range(1, LG):
         states(g)
-        finish_all(g)
+        finish_far(g)
+    for g in range(LG):
+        finish_send(2, 1 - k, other, g)
+    for g in range(LG):
+        finish(k, g, gg.at[own_j, g], False)
 
     wo_copy.wait()
     res_copy.wait()
@@ -541,10 +547,24 @@
         local(xo.at[1 - k, pl.ds(0, ROWS), cols], out.at[:, cols], L_OUT + n).wait()
 
 
+COPIES = 4
+
+
+def place(src, out, sems):
+    part = ROWS // COPIES
+    copies = []
+    for i in range(COPIES):
+        rows = pl.ds(i * part, part)
+        copies.append(pltpu.make_async_copy(src.at[rows], out.at[rows], sems.at[i]))
+        copies[-1].start()
+    for cp in copies:
+        cp.wait()
+
+
 def shards(tokens, norm_gain, w_in, short_weight, conv_bias, decay_rates, residues, w_out):
     vmem = pl.BlockSpec(memory_space=pltpu.VMEM)
     hbm = pl.BlockSpec(memory_space=pl.ANY)
-    return pl.pallas_call(
+    mixed = pl.pallas_call(
         kernel,
         out_shape=jax.ShapeDtypeStruct((ROWS, WIDTH), BF),
         in_specs=[hbm, vmem, hbm, vmem, vmem, vmem, vmem, hbm],
@@ -592,6 +612,13 @@
         residues,
         w_out,
     )
+    return pl.pallas_call(
+        place,
+        out_shape=jax.ShapeDtypeStruct((ROWS, WIDTH), BF),
+        in_specs=[vmem],
+        out_specs=hbm,
+        scratch_shapes=[pltpu.SemaphoreType.DMA((COPIES,))],
+    )(mixed)
 
 
 def solution(mesh):

time: 92 us -> 90.9 us (0.988)
  local copies, waits for them, and re-layouts: 3.91 us -> 0 us
  Pallas kernels: 87.9 us -> 90.5 us
    unnamed x1 -> x0, local copies, waits for them, and re-layouts: 3.91 us -> none
    pallas_call x0 -> x1, Pallas kernels: none -> 3.58 us  [shards(): pl.pallas_call(place, out_shape=jax.ShapeDtypeStruct((ROWS, WIDTH), BF),...]
    pallas_call x1, Pallas kernels: 87.9 us -> 86.9 us  [shards(): pl.pallas_call(kernel, out_shape=jax.ShapeDtypeStruct((ROWS, WIDTH), BF),...]
where the time goes in v3:
time: 90.9 us; the launch traced here: 90.7 us
  Pallas kernels  90.5 us (100%)
    pallas_call x1, Pallas kernels, shards(): pl.pallas_call(kernel, out_shape=jax.ShapeDtypeStruct((ROWS, WIDTH), BF),...  86.9 us
    pallas_call x1, Pallas kernels, shards(): pl.pallas_call(place, out_shape=jax.ShapeDtypeStruct((ROWS, WIDTH), BF),...  3.58 us

profile of v3, /device:TPU:1, one launch (start us, length us, event | category | flops | bytes accessed | tf_op | source)
XLA Modules:
  0.0 90.7 jit_solution(9251286172791210916)
XLA Ops:
  0.0 86.9 %shard_map.82.src = bf16[384,4096]{1,0:T(8,128)(2,1)} custom-call(bf16[384,4096]{1,0:T(8,128)(2,1)} %tok.1, bf16[32,128]{1,0:T(8,128)(2,1)} %bitcast.6, bf16[3,4096,512]{2,1,0:T(8,128)(2,1)} %bitcast.4, bf16[3,7,512]{2,1,0:T(8,128)(2,1)} %bitcast.5, f32[1,512]{1,0:T(1,128)} %bitcast.7, f32[16,512]{1,0:T(8,128)} %decay.1, f32[16,512]{1,0:T(8,128)} %resid.1, ...), custom_call_target="tpu_custom_call" | custom-call | flops 25999998976 | bytes 26214400 | tf_op jit(solution)/shard_map/pallas_call | solution.py:567
  86.9 3.6 %shard_map.83 = bf16[384,4096]{1,0:T(8,128)(2,1)} custom-call(bf16[384,4096]{1,0:T(8,128)(2,1)} %shard_map.82.src), custom_call_target="tpu_custom_call" | custom-call | tf_op jit(solution)/shard_map/pallas_call | solution.py:615

commit v4 on v3

--- a/solution.py
+++ b/solution.py
@@ -9,7 +9,7 @@
 
 MESH = pl.DeviceIdType.MESH
 BF, F32 = jnp.bfloat16, jnp.float32
-STATE = F32
+STATE = BF
 
 ROWS = 384
 HALO = 16
@@ -547,18 +547,22 @@
         local(xo.at[1 - k, pl.ds(0, ROWS), cols], out.at[:, cols], L_OUT + n).wait()
 
 
-COPIES = 4
-
-
-def place(src, out, sems):
+COPIES = 8
+
+
+def place(src, out, held, first, second):
     part = ROWS // COPIES
-    copies = []
+    loads, stores = [], []
     for i in range(COPIES):
         rows = pl.ds(i * part, part)
-        copies.append(pltpu.make_async_copy(src.at[rows], out.at[rows], sems.at[i]))
-        copies[-1].start()
-    for cp in copies:
-        cp.wait()
+        loads.append(pltpu.make_async_copy(src.at[rows], held.at[rows], first.at[i]))
+        stores.append(pltpu.make_async_copy(held.at[rows], out.at[rows], second.at[i]))
+        loads[-1].start()
+    for load, store in zip(loads, stores):
+        load.wait()
+        store.start()
+    for store in stores:
+        store.wait()
 
 
 def shards(tokens, norm_gain, w_in, short_weight, conv_bias, decay_rates, residues, w_out):
@@ -615,9 +619,13 @@
     return pl.pallas_call(
         place,
         out_shape=jax.ShapeDtypeStruct((ROWS, WIDTH), BF),
-        in_specs=[vmem],
+        in_specs=[hbm],
         out_specs=hbm,
-        scratch_shapes=[pltpu.SemaphoreType.DMA((COPIES,))],
+        scratch_shapes=[
+            pltpu.VMEM((ROWS, WIDTH), BF),
+            pltpu.SemaphoreType.DMA((COPIES,)),
+            pltpu.SemaphoreType.DMA((COPIES,)),
+        ],
     )(mixed)
 
 

time: 90.9 us -> 89.3 us (0.982)
  Pallas kernels: 90.5 us -> 88.9 us
where the time goes in v4:
time: 89.3 us; the launch traced here: 89.1 us
  Pallas kernels  88.9 us (100%)
    pallas_call x1, Pallas kernels, shards(): pl.pallas_call(kernel, out_shape=jax.ShapeDtypeStruct((ROWS, WIDTH), BF),...  86.1 us
    pallas_call x1, Pallas kernels, shards(): pl.pallas_call(place, out_shape=jax.ShapeDtypeStruct((ROWS, WIDTH), BF),...  2.79 us

profile of v4, /device:TPU:1, one launch (start us, length us, event | category | flops | bytes accessed | tf_op | source)
XLA Modules:
  0.0 89.1 jit_solution(10658926412337306894)
XLA Ops:
  0.0 86.1 %shard_map.82.src = bf16[384,4096]{1,0:T(8,128)(2,1)} custom-call(bf16[384,4096]{1,0:T(8,128)(2,1)} %tok.1, bf16[32,128]{1,0:T(8,128)(2,1)} %bitcast.6, bf16[3,4096,512]{2,1,0:T(8,128)(2,1)} %bitcast.4, bf16[3,7,512]{2,1,0:T(8,128)(2,1)} %bitcast.5, f32[1,512]{1,0:T(1,128)} %bitcast.7, f32[16,512]{1,0:T(8,128)} %decay.1, f32[16,512]{1,0:T(8,128)} %resid.1, ...), custom_call_target="tpu_custom_call" | custom-call | flops 25999998976 | bytes 26214400 | tf_op jit(solution)/shard_map/pallas_call | solution.py:571
  86.1 2.8 %shard_map.83 = bf16[384,4096]{1,0:T(8,128)(2,1)} custom-call(bf16[384,4096]{1,0:T(8,128)(2,1)} %shard_map.82.src), custom_call_target="tpu_custom_call" | custom-call | tf_op jit(solution)/shard_map/pallas_call | solution.py:619
